TPU v7x, 32 devices: a whole 2x2x4 slice. The times are simulated.
32 devices in a mesh: groups: 2 (over y), job: 4 (over x, core), tensor: 4 (over z).
Axes of the slice: x: 2, y: 2, z: 4, core: 2. Of those that a mesh axis runs over, the one named last changes fastest.
Arguments:
- tokens: bfloat16 [16384, 8192], P(('groups', 'job'), 'tensor'), parts along dimension 0, may hold values from -6 to 6
- weight: bfloat16 [8192, 1024], P('tensor'), may hold values from -0.0625 to 0.0625
- dequant_scale: float32 [1024], P('tensor'), may hold values from 0.5 to 4
- down_factor: bfloat16 [32, 64, 8192], P(('groups', 'job'), None, 'tensor'), parts along dimension 0, may hold values from -0.0625 to 0.0625
- up_factor: bfloat16 [32, 64, 1024], P(('groups', 'job'), None, 'tensor'), parts along dimension 0, may hold values from -0.75 to 0.75
- counts: int32 [32], P(('groups', 'job')), parts along dimension 0, may hold values from 1 to 2045, as said below
- job_adapter: int32 [32], P(('groups', 'job')), parts along dimension 0, may hold values from 0 to 3
- cotangent: bfloat16 [16384, 1024], P(('groups', 'job'), 'tensor'), parts along dimension 0, may hold values from -6 to 6
Outputs:
- mixed: bfloat16 [16384, 1024], P(('groups', 'job'), 'tensor'), parts along dimension 0
- token_gradient: bfloat16 [16384, 8192], P(('groups', 'job'), 'tensor'), parts along dimension 0
- down_gradient: float32 [32, 64, 8192], P(('groups', 'job'), None, 'tensor'), parts along dimension 0
- up_gradient: float32 [32, 64, 1024], P(('groups', 'job'), None, 'tensor'), parts along dimension 0
There are 2 independent parts, one for each index of `groups`. A program takes and returns all parts, laid end to end along the dimension named above; an argument that names none is the same for every part. Nothing has to cross between parts.
Inputs may be any that keep to these rules, and one draw needn't show every extreme that they name: Each count is 1 or more; the 4 counts of one index of job sum to at most 2048, and at some index of job to exactly 2048.
All inputs are finite; a program needn't handle non-finite values.
Results may differ from a plain program's by a relative error of at most 0.013.
Values may be sent and summed in bfloat16 or wider, within the bound.
A program may use at most 128 MiB of HBM per device.

v0:
```python
import jax
import jax.numpy as jnp
from jax import lax
from jax.sharding import PartitionSpec as P

BLK = 128


ADAPTER_SCALE = 2.0


def selection(counts, job_adapter, token_rows):
    bounds = jnp.cumsum(counts)
    starts = bounds - counts
    position = lax.broadcasted_iota(jnp.int32, (token_rows, 1), 0)
    owned = ((position >= starts[None, :]) & (position < bounds[None, :])).astype(jnp.float32)
    slot_ids = lax.broadcasted_iota(jnp.int32, (1, counts.shape[0]), 1)
    table = (job_adapter[:, None] == slot_ids).astype(jnp.float32)
    select = jnp.dot(owned, table, precision=lax.Precision.HIGHEST)
    return (select, jnp.sum(owned, axis=1))


def apply_live(items, item_live, work, out_width, kind):
    flat_live = item_live.reshape(-1).astype(jnp.int32)
    total = jnp.sum(flat_live)
    order = jnp.argsort(1 - flat_live, stable=True)
    flat_items = items.reshape((-1,) + items.shape[2:])
    start = jnp.zeros((flat_items.shape[0], flat_items.shape[1], out_width), kind)

    def step(count, acc):
        where = order[count]
        piece = lax.dynamic_index_in_dim(flat_items, where, 0, keepdims=False)
        return lax.dynamic_update_index_in_dim(acc, work(piece).astype(kind), where, 0)

    result = lax.fori_loop(0, total, step, start)
    return result.reshape(items.shape[:2] + result.shape[1:])


def reduce_parts(partial_value):
    return lax.psum_scatter(
        partial_value.astype(jnp.bfloat16), "tensor", scatter_dimension=3, tiled=True
    ).astype(jnp.float32)


def full_rows(blocks):
    return lax.all_gather(blocks, "tensor", axis=3, tiled=True)


def local(tokens, weight, dequant_scale, down_factor, up_factor, counts, job_adapter, cotangent):
    peers = lax.axis_size("job")
    token_rows, width_portion = tokens.shape
    adapters, rank, _ = down_factor.shape
    out_part = up_factor.shape[2]
    out_width = weight.shape[1]
    stacks = token_rows // BLK // peers
    cross = (((1,), (1,)), ((), ()))
    select, active_mask = selection(counts, job_adapter, token_rows)
    down_factor_table = down_factor.reshape(adapters * rank, width_portion)
    up_factor_table = up_factor.reshape(adapters * rank, out_part)
    low_part = lax.dot_general(tokens, down_factor_table, cross, preferred_element_type=jnp.float32)
    masked_upstream = (cotangent.astype(jnp.float32) * active_mask[:, None]).astype(jnp.bfloat16)
    grad_part = lax.dot_general(
        masked_upstream, up_factor_table, cross, preferred_element_type=jnp.float32
    )
    wide = jnp.repeat(select, rank, axis=1)
    reduced_rows = (
        lax.psum(low_part.astype(jnp.bfloat16), "tensor").astype(jnp.float32) * wide
    ).astype(jnp.bfloat16)
    gradient_rows = (
        lax.psum(grad_part.astype(jnp.bfloat16), "tensor").astype(jnp.float32) * wide
    ).astype(jnp.bfloat16)
    scaled_cot = (
        cotangent.astype(jnp.float32) * dequant_scale[None, :] * active_mask[:, None]
    ).astype(jnp.bfloat16)
    token_blocks = tokens.reshape(stacks, peers, BLK, width_portion)
    cot_blocks = scaled_cot.reshape(stacks, peers, BLK, out_part)

    def forward_piece(piece):
        return jnp.dot(piece, weight, preferred_element_type=jnp.float32)

    def backward_piece(piece):
        return lax.dot_general(piece, weight, cross, preferred_element_type=jnp.float32)

    block_ids = lax.broadcasted_iota(jnp.int32, (stacks, peers), 0) * peers
    column_ids = lax.broadcasted_iota(jnp.int32, (stacks, peers), 1)
    here = lax.axis_index("job")
    loads = lax.all_gather(counts, "job", axis=0, tiled=True)
    source_rows = jnp.sum(loads.reshape(peers, -1), axis=1)
    source_blocks = (source_rows + BLK - 1) // BLK
    home_block = block_ids + jnp.mod(here - column_ids, peers)
    item_live = home_block < source_blocks[None, :]
    moved = lax.all_to_all(
        jnp.roll(token_blocks, here, axis=1), "job", split_axis=1, concat_axis=1, tiled=True
    )
    partial_value = apply_live(moved, item_live, forward_piece, out_width, jnp.float32)
    summed = (reduce_parts(partial_value) * dequant_scale).astype(jnp.bfloat16)
    base = jnp.roll(
        lax.all_to_all(summed, "job", split_axis=1, concat_axis=1, tiled=True), -here, axis=1
    )
    arrived = full_rows(
        lax.all_to_all(
            jnp.roll(cot_blocks, here, axis=1), "job", split_axis=1, concat_axis=1, tiled=True
        )
    )
    back_part = apply_live(arrived, item_live, backward_piece, width_portion, jnp.bfloat16)
    frozen_gradient = jnp.roll(
        lax.all_to_all(back_part, "job", split_axis=1, concat_axis=1, tiled=True), -here, axis=1
    )
    frozen_rows = base.reshape(token_rows, out_part).astype(jnp.float32)
    adapter_rows = jnp.dot(reduced_rows, up_factor_table, preferred_element_type=jnp.float32)
    mixed = ((frozen_rows + ADAPTER_SCALE * adapter_rows) * active_mask[:, None]).astype(
        jnp.bfloat16
    )
    adapter_gradient = jnp.dot(gradient_rows, down_factor_table, preferred_element_type=jnp.float32)
    token_gradient = (
        frozen_gradient.reshape(token_rows, width_portion).astype(jnp.float32)
        + ADAPTER_SCALE * adapter_gradient
    ).astype(jnp.bfloat16)
    along_rows = (((0,), (0,)), ((), ()))
    down_gradient = ADAPTER_SCALE * lax.dot_general(
        gradient_rows, tokens, along_rows, preferred_element_type=jnp.float32
    )
    up_gradient = ADAPTER_SCALE * lax.dot_general(
        reduced_rows, masked_upstream, along_rows, preferred_element_type=jnp.float32
    )
    return (
        mixed,
        token_gradient,
        down_gradient.reshape(adapters, rank, width_portion),
        up_gradient.reshape(adapters, rank, out_part),
    )


def solution(mesh):
    placed = (
        P(("groups", "job"), "tensor"),
        P("tensor", None),
        P("tensor"),
        P(("groups", "job"), None, "tensor"),
        P(("groups", "job"), None, "tensor"),
        P(("groups", "job")),
        P(("groups", "job")),
        P(("groups", "job"), "tensor"),
    )
    return jax.shard_map(
        local,
        mesh=mesh,
        in_specs=placed,
        out_specs=(
            P(("groups", "job"), "tensor"),
            P(("groups", "job"), "tensor"),
            P(("groups", "job"), None, "tensor"),
            P(("groups", "job"), None, "tensor"),
        ),
        check_vma=False,
    )
```

profile of v0, /device:TPU:0, one launch (start us, length us, event | category | flops | bytes accessed | tf_op | source)
XLA Modules:
  0.0 465.7 jit_solution(18156539666905899500)
XLA Ops:
  11.0 18.5 %all_to_all.20 = bf16[4,4,128,256]{3,2,0,1:T(8,128)(2,1)S(1)} all-to-all(bf16[4,4,128,256]{3,2,0,1:T(8,128)(2,1)S(1)} %copy.44), channel_id=1, replica_groups=mesh['groups'=2,'job'=4,'tensor'=4] {'job'}, dimensions={1} | all-to-all | bytes 2097152 | tf_op jit(solution)/shard_map/all_to_all | solution.py:101
  30.5 8.3 %fusion.12 = bf16[4,4,128,2048]{3,2,1,0:T(8,128)(2,1)} fusion(s32[]{:T(128)S(6)} %select_n.62, bf16[4,4,128,2048]{3,2,1,0:T(8,128)(2,1)} %bitcast.62), kind=kLoop, calls=%fused_computation.19 | loop fusion | flops 4194304 | bytes 16777220 | tf_op jit(solution)/shard_map/jit(_roll_dynamic)/concatenate | solution.py:93
  38.8 8.5 %copy.32 = bf16[4,4,128,2048]{3,2,0,1:T(8,128)(2,1)} copy(bf16[4,4,128,2048]{3,2,1,0:T(8,128)(2,1)} %fusion.12) | data formatting | bytes 16777216 | tf_op jit(solution)/shard_map/jit(_roll_dynamic)/dynamic_slice | solution.py:93
  47.3 5.8 %all-to-all-start = ((bf16[4,4,128,2048]{3,2,0,1:T(8,128)(2,1)}), bf16[4,4,128,2048]{3,2,0,1:T(8,128)(2,1)}, u32[]{:S(2)}, u32[]{:S(2)}) async-start(bf16[4,4,128,2048]{3,2,0,1:T(8,128)(2,1)} %copy.32), calls=%async_computation | async-start | bytes 16777216 | tf_op jit(solution)/shard_map/all_to_all | solution.py:92
  54.6 6.8 %convolution_convert_fusion.2 = bf16[2048,256]{1,0:T(8,128)(2,1)} fusion(bf16[2048,2048]{1,0:T(8,128)(2,1)} %param.16, bf16[256,2048]{1,0:T(8,128)(2,1)S(1)} %bitcast.60), kind=kOutput, calls=%fused_computation.28 | convolution fusion | flops 2148007936 | bytes 10485760 | tf_op jit(solution)/shard_map/dot_general | solution.py:60
  63.1 83.2 %all-reduce = s32[16]{0:T(128)S(1)} all-reduce(s32[16]{0:T(128)S(1)} %dynamic-update-slice), channel_id=1, replica_groups=mesh['groups'=2,'job'=4,'tensor'=4] {'job'}, use_global_device_ids=true, to_apply=%add | all-reduce | flops 16 | bytes 128
  148.9 8.5 %copy.33 = bf16[4,4,128,2048]{3,2,1,0:T(8,128)(2,1)} copy(bf16[4,4,128,2048]{3,2,0,1:T(8,128)(2,1)} %all-to-all-done) | data formatting | bytes 16777216 | tf_op jit(solution)/shard_map/all_to_all | solution.py:92
  159.9 71.5 %while.20 = (s32[]{:T(128)}, bf16[16,128,1024]{2,1,0:T(8,128)(2,1)}, s32[]{:T(128)}, s32[16]{0:T(128)S(1)}, bf16[16,128,2048]{2,1,0:T(8,128)(2,1)}, /*index=5*/b...) while((s32[]{:T(128)}, bf16[16,128,1024]{2,1,0:T(8,128)(2,1)}, s32[]{:T(128)}, s32[16]{0:T(128)S(1)}, ...), condition=%wide.region_4.6_spmd, body=%wide.region_3.5_spmd.sunk | while | flops 536870912 | bytes 5244077 | solution.py:35
  235.9 79.2 %while.21 = (s32[]{:T(128)}, bf16[16,128,2048]{2,1,0:T(8,128)(2,1)}, s32[]{:T(128)}, s32[16]{0:T(128)S(1)}, bf16[16,128,1024]{2,1,0:T(8,128)(2,1)}, /*index=5*/b...) while((s32[]{:T(128)}, bf16[16,128,2048]{2,1,0:T(8,128)(2,1)}, s32[]{:T(128)}, s32[16]{0:T(128)S(1)}, ...), condition=%wide.region_10.13_spmd, body=%wide.region_9.12_spmd.sunk | while | flops 537133056 | bytes 4981933 | solution.py:35
  239.2 4.6 fusion.51
  247.0 4.6 fusion.51
  254.9 4.6 fusion.51
  262.7 4.6 fusion.51
  270.6 4.6 fusion.51
  286.3 4.6 fusion.51
  301.9 4.7 %fusion.51 = bf16[16,128,2048]{2,1,0:T(8,128)(2,1)} fusion(bf16[16,128,2048]{2,1,0:T(8,128)(2,1)} %get-tuple-element.219, s32[]{:T(128)S(6)} %select_n.87, bf16[2048,1024]{1,0:T(8,128)(2,1)} %get-tuple-element.232, bf16[16,128,1024]{2,1,0:T(8,128)(2,1)} %get-tuple-element.231), kind=kOutput, calls=%fused_computation.7.clone.1 | convolution fusion | flops 537133056 | bytes 4981760 | tf_op jit(solution)/shard_map/while/body/dot_general | solution.py:82
  315.2 8.3 %copy.40 = bf16[4,4,128,2048]{3,2,0,1:T(8,128)(2,1)} copy(bf16[4,4,128,2048]{3,2,1,0:T(8,128)(2,1)} %bitcast.63) | data formatting | bytes 16777216 | tf_op jit(solution)/shard_map/reshape | solution.py:36
  323.4 6.0 %all-to-all-start.3 = ((bf16[4,4,128,2048]{3,2,0,1:T(8,128)(2,1)}), bf16[4,4,128,2048]{3,2,0,1:T(8,128)(2,1)}, u32[]{:S(2)}, u32[]{:S(2)}) async-start(bf16[4,4,128,2048]{3,2,0,1:T(8,128)(2,1)} %copy.40), calls=%async_computation.4 | async-start | bytes 16777216 | tf_op jit(solution)/shard_map/all_to_all | solution.py:107
  336.4 7.1 %convolution_multiply_fusion = f32[256,2048]{1,0:T(8,128)} fusion(bf16[2048,2048]{1,0:T(8,128)(2,1)} %param.16, f32[2048,256]{1,0:T(8,128)S(1)} %copy.36, bf16[2048,256]{1,0:T(8,128)(2,1)S(1)} %copy-done.2), kind=kOutput, calls=%fused_computation.20 | convolution fusion | flops 2149580800 | bytes 13631488 | tf_op jit(solution)/shard_map/dot_general | solution.py:120
  343.4 79.0 %all-to-all-done.3 = bf16[4,4,128,2048]{3,2,0,1:T(8,128)(2,1)} async-done(((bf16[4,4,128,2048]{3,2,0,1:T(8,128)(2,1)}), bf16[4,4,128,2048]{3,2,0,1:T(8,128)(2,1)}, u32[]{:S(2)}, u32[]{:S(2)}) %all-to-all-start.3) | async-done | bytes 8388640 | tf_op jit(solution)/shard_map/all_to_all | solution.py:107
  422.4 6.0 %fusion.11 = f32[4,4,128,2048]{3,2,0,1:T(8,128)S(1)} fusion(s32[]{:T(128)S(6)} %select_n.64, bf16[4,4,128,2048]{3,2,0,1:T(8,128)(2,1)} %all-to-all-done.3), kind=kLoop, calls=%fused_computation.18 | loop fusion | flops 8388608 | bytes 25165828 | tf_op jit(solution)/shard_map/convert_element_type | solution.py:116
  428.4 6.0 %copy.41 = f32[4,4,128,2048]{3,2,1,0:T(8,128)} copy(f32[4,4,128,2048]{3,2,0,1:T(8,128)S(1)} %fusion.11) | data formatting | bytes 33554432 | tf_op jit(solution)/shard_map/convert_element_type | solution.py:116
  441.2 9.8 %fusion.9 = bf16[2048,2048]{1,0:T(8,128)(2,1)} fusion(f32[4,4,128,2048]{3,2,1,0:T(8,128)} %copy.41, bf16[256,2048]{1,0:T(8,128)(2,1)S(1)} %bitcast.61, f32[2048,256]{1,0:T(8,128)S(1)} %copy.36, bf16[2048,256]{1,0:T(8,128)(2,1)} %get-tuple-element.101), kind=kOutput, calls=%fused_computation.16 | convolution fusion | flops 2161639424 | bytes 29360128 | tf_op jit(solution)/shard_map/dot_general | solution.py:114
  451.0 4.7 %all-to-all-done.1 = bf16[4,4,128,256]{3,2,0,1:T(8,128)(2,1)} async-done(((bf16[4,4,128,256]{3,2,0,1:T(8,128)(2,1)}), bf16[4,4,128,256]{3,2,0,1:T(8,128)(2,1)}, u32[]{:S(2)}, u32[]{:S(2)}) %all-to-all-start.1) | async-done | bytes 1048608 | tf_op jit(solution)/shard_map/all_to_all | solution.py:98
  (100 shorter events, 98.2 us)
Async XLA Ops:
  7.2 47.5 %copy-start = (bf16[4,64,2048]{2,1,0:T(8,128)(2,1)S(1)}, bf16[4,64,2048]{2,1,0:T(8,128)(2,1)}, u32[]{:S(2)}) copy-start(bf16[4,64,2048]{2,1,0:T(8,128)(2,1)} %param.19) | copy-start | bytes 3145732
  7.2 224.3 %all-gather.2.cloned.1.call-start = ((), (), s32[]{:S(2)}) async-start(), calls=%async_computation.6 | async-start | bytes 5242880 | tf_op jit(solution)/shard_map/all_gather | solution.py:46
  47.3 5.8 %copy-start.1 = (bf16[2048,256]{1,0:T(8,128)(2,1)S(1)}, bf16[2048,256]{1,0:T(8,128)(2,1)}, u32[]{:S(2)}) copy-start(bf16[2048,256]{1,0:T(8,128)(2,1)} %param.23) | copy-start | bytes 3145732
  47.3 5.8 %copy-start.4 = (bf16[4,64,256]{2,1,0:T(8,128)(2,1)S(1)}, bf16[4,64,256]{2,1,0:T(8,128)(2,1)}, u32[]{:S(2)}) copy-start(bf16[4,64,256]{2,1,0:T(8,128)(2,1)} %param.20) | copy-start | bytes 393220
  47.3 101.6 %all-to-all-start = ((bf16[4,4,128,2048]{3,2,0,1:T(8,128)(2,1)}), bf16[4,4,128,2048]{3,2,0,1:T(8,128)(2,1)}, u32[]{:S(2)}, u32[]{:S(2)}) async-start(bf16[4,4,128,2048]{3,2,0,1:T(8,128)(2,1)} %copy.32), calls=%async_computation | async-start | bytes 16777216 | tf_op jit(solution)/shard_map/all_to_all | solution.py:92
  53.1 280.1 %all-reduce.4.cloned.1.call-start = ((), (), s32[]{:S(2)}) async-start(), calls=%async_computation.7 | async-start | bytes 4194304 | tf_op jit(solution)/shard_map/psum | solution.py:67
  54.6 6.9 %copy-start.8 = (u32[32]{0:T(128)S(1)}, u32[32]{0:T(128)}, u32[]{:S(2)}) copy-start(u32[32]{0:T(128)} %constant.123) | copy-start | bytes 388
  54.6 8.2 %copy-start.6 = (s32[4]{0:T(128)S(1)}, s32[4]{0:T(128)}, u32[]{:S(2)}) copy-start(s32[4]{0:T(128)} %param.21) | copy-start | bytes 52
  61.5 372.9 %reduce-scatter.2.cloned.1.call-start = ((), (), s32[]{:S(2)}) async-start(), calls=%async_computation.5 | async-start | bytes 5242880 | tf_op jit(solution)/shard_map/reduce_scatter | solution.py:40
  323.4 6.0 %copy-start.7 = (s32[4]{0:T(128)S(1)}, s32[4]{0:T(128)}, u32[]{:S(2)}) copy-start(s32[4]{0:T(128)} %param.22) | copy-start | bytes 52
  323.4 99.0 %all-to-all-start.3 = ((bf16[4,4,128,2048]{3,2,0,1:T(8,128)(2,1)}), bf16[4,4,128,2048]{3,2,0,1:T(8,128)(2,1)}, u32[]{:S(2)}, u32[]{:S(2)}) async-start(bf16[4,4,128,2048]{3,2,0,1:T(8,128)(2,1)} %copy.40), calls=%async_computation.4 | async-start | bytes 16777216 | tf_op jit(solution)/shard_map/all_to_all | solution.py:107
  333.2 3.2 copy-start.2
  428.4 6.0 %copy-start.5 = (f32[256]{0:T(256)S(1)}, f32[256]{0:T(256)}, u32[]{:S(2)}) copy-start(f32[256]{0:T(256)} %param.18) | copy-start | bytes 3076
  436.9 18.8 %all-to-all-start.1 = ((bf16[4,4,128,256]{3,2,0,1:T(8,128)(2,1)}), bf16[4,4,128,256]{3,2,0,1:T(8,128)(2,1)}, u32[]{:S(2)}, u32[]{:S(2)}) async-start(bf16[4,4,128,256]{3,2,0,1:T(8,128)(2,1)} %copy.34), calls=%async_computation.2 | async-start | bytes 2097152 | tf_op jit(solution)/shard_map/all_to_all | solution.py:98
  455.7 2.0 copy-start.3
Sparse Core Ops, SparseCore 0:
  30.6 80.8 all-gather.1
  114.5 85.2 all-reduce.3
  231.5 77.0 reduce-scatter.1
where the time goes:
time: 457 us; the launch traced here: 466 us
  matrix products  114 us (25%)
  blocking collectives  102 us (22%)
  waiting for transfers between devices  83.8 us (18%)
  local copies, waits for them, and re-layouts  57.7 us (13%)
  loops' own time  54.1 us (12%)
  other arithmetic  23.3 us (5%)
  starting transfers between devices  16.1 us (4%)
  between operations  14.7 us (3%)
    unnamed x1, blocking collectives  83.2 us
    all_to_all x1, waiting for transfers between devices, local(): lax.all_to_all(back_part, 'job', split_axis=1, concat_axis=1, tiled=True)  79 us
    another operation x2, loops' own time, apply_live(): result = lax.fori_loop(0, total, step, start)  54.1 us
    dot_general x10, matrix products, backward_piece(): lax.dot_general(piece, weight, cross, preferred_element_type=jnp.float32)  46.1 us
    dot_general x10, matrix products, forward_piece(): return jnp.dot(piece, weight, preferred_element_type=jnp.float32)  38.1 us
    all_to_all x1, blocking collectives, local(): lax.all_to_all(jnp.roll(cot_blocks, here, axis=1), 'job', split_axis=1, c...  18.5 us
    dynamic_slice x20, local copies, waits for them, and re-layouts, step(): where = order[count]  12.4 us
    dot_general x1, matrix products, local(): jnp.dot(gradient_rows, down_factor_table, preferred_element_type=jnp.floa...  9.81 us
  transfers between devices with their start and end apart: 6, of which 2 were waited for; matrix products, arithmetic and copies ran while one was open for 40% of the time, Pallas kernels for 0%

commit v1 on v0

v1 whole, which is shorter than its diff:
```python
import jax
import jax.numpy as jnp
from jax import lax
from jax.sharding import PartitionSpec as P

ADAPTER_SCALE = 2.0


def selection(counts, job_adapter, token_rows):
    bounds = jnp.cumsum(counts)
    starts = bounds - counts
    position = lax.broadcasted_iota(jnp.int32, (token_rows, 1), 0)
    owned = (position >= starts[None, :]) & (position < bounds[None, :])
    slot = jnp.sum(jnp.where(owned, job_adapter[None, :] + 1, 0), axis=1, keepdims=True) - 1
    return slot


def local(tokens, weight, dequant_scale, down_factor, up_factor, counts, job_adapter, cotangent):
    token_rows, width_portion = tokens.shape
    adapters, rank, _ = down_factor.shape
    out_part = up_factor.shape[2]
    cross = (((1,), (1,)), ((), ()))
    along_rows = (((0,), (0,)), ((), ()))
    slot = selection(counts, job_adapter, token_rows)
    live = slot >= 0
    down_table = down_factor.reshape(adapters * rank, width_portion)
    up_table = up_factor.reshape(adapters * rank, out_part)
    masked = jnp.where(live, cotangent, 0)
    scaled = jnp.where(live, cotangent.astype(jnp.float32) * dequant_scale[None, :], 0.0).astype(
        jnp.bfloat16
    )
    every = lax.all_gather(scaled, "tensor", axis=1, tiled=True)

    def own_slot(full):
        total = jnp.zeros((token_rows, rank), jnp.float32)
        for a in range(adapters):
            total = jnp.where(slot == a, full[:, a * rank : (a + 1) * rank], total)
        return total.astype(jnp.bfloat16)

    def spread(compact):
        return jnp.concatenate([jnp.where(slot == a, compact, 0) for a in range(adapters)], axis=1)

    low = own_slot(lax.dot_general(tokens, down_table, cross, preferred_element_type=jnp.float32))
    grad = own_slot(lax.dot_general(masked, up_table, cross, preferred_element_type=jnp.float32))
    both = lax.psum(jnp.concatenate([low, grad], axis=1), "tensor")
    low_rows = spread(both[:, :rank])
    grad_rows = spread(both[:, rank:])
    part = jnp.dot(tokens, weight, preferred_element_type=jnp.float32).astype(jnp.bfloat16)
    base = lax.psum_scatter(part, "tensor", scatter_dimension=1, tiled=True)
    back = lax.dot_general(every, weight, cross, preferred_element_type=jnp.float32)
    token_gradient = (
        back
        + ADAPTER_SCALE * jnp.dot(grad_rows, down_table, preferred_element_type=jnp.float32)
    ).astype(jnp.bfloat16)
    down_gradient = ADAPTER_SCALE * lax.dot_general(
        grad_rows, tokens, along_rows, preferred_element_type=jnp.float32
    )
    up_gradient = ADAPTER_SCALE * lax.dot_general(
        low_rows, masked, along_rows, preferred_element_type=jnp.float32
    )
    base_scaled = base.astype(jnp.float32) * dequant_scale[None, :]
    mixed = jnp.where(
        live,
        base_scaled
        + ADAPTER_SCALE * jnp.dot(low_rows, up_table, preferred_element_type=jnp.float32),
        0.0,
    ).astype(jnp.bfloat16)
    return (
        mixed,
        token_gradient,
        down_gradient.reshape(adapters, rank, width_portion),
        up_gradient.reshape(adapters, rank, out_part),
    )


def solution(mesh):
    placed = (
        P(("groups", "job"), "tensor"),
        P("tensor", None),
        P("tensor"),
        P(("groups", "job"), None, "tensor"),
        P(("groups", "job"), None, "tensor"),
        P(("groups", "job")),
        P(("groups", "job")),
        P(("groups", "job"), "tensor"),
    )
    return jax.shard_map(
        local,
        mesh=mesh,
        in_specs=placed,
        out_specs=(
            P(("groups", "job"), "tensor"),
            P(("groups", "job"), "tensor"),
            P(("groups", "job"), None, "tensor"),
            P(("groups", "job"), None, "tensor"),
        ),
        check_vma=False,
    )
```

time: 457 us -> 227 us (0.50); the launches traced: 466 us -> 227 us
  blocking collectives: 102 us -> 0 us
  waiting for transfers between devices: 83.8 us -> 152 us
  matrix products: 114 us -> 56.1 us
  local copies, waits for them, and re-layouts: 57.7 us -> 0.06 us
  loops' own time: 54.1 us -> 0 us
  other arithmetic: 23.3 us -> 5.32 us
  starting transfers between devices: 16.1 us -> 0.3 us
    all_to_all x3 -> x0, waiting for transfers between devices: 83.7 us -> none  [the longest x1 79 us: local(): lax.all_to_all(back_part, 'job', split_axis=1, concat_axis=1, tiled=True)]
    unnamed x1 -> x0, blocking collectives: 83.2 us -> none
    all_gather x1, waiting for transfers between devices: 0.02 us -> 73.1 us  [local(): every = lax.all_gather(scaled, 'tensor', axis=1, tiled=True)]
    dot_general x27 -> x8, matrix products: 114 us -> 56.1 us  [the longest x1 15.3 us: local(): lax.dot_general(every, weight, cross, preferred_element_type=jnp.float32)]
    another operation x2 -> x0, loops' own time: 54.1 us -> none  [apply_live(): result = lax.fori_loop(0, total, step, start)]
    reduce_scatter x1, waiting for transfers between devices: 0.01 us -> 52.6 us  [local(): base = lax.psum_scatter(part, 'tensor', scatter_dimension=1, tiled=True)]
    psum x1, waiting for transfers between devices: 0.02 us -> 25.8 us  [local(): both = lax.psum(jnp.concatenate([low, grad], axis=1), 'tensor')]
    dynamic_slice x21 -> x0, local copies, waits for them, and re-layouts: 20.9 us -> none  [the longest x20 12.4 us: step(): where = order[count]]
  transfers between devices with their start and end apart: 6 -> 3, of which waited for: 2 -> 3; matrix products, arithmetic and copies ran while one was open for 40% -> 22% of each run, Pallas kernels for 0% -> 0%
where the time goes in v1:
time: 227 us
  waiting for transfers between devices  152 us (67%)
  matrix products  56.1 us (25%)
  between operations  13.9 us (6%)
  other arithmetic  5.32 us (2%)
    all_gather x1, waiting for transfers between devices, local(): every = lax.all_gather(scaled, 'tensor', axis=1, tiled=True)  73.1 us
    reduce_scatter x1, waiting for transfers between devices, local(): base = lax.psum_scatter(part, 'tensor', scatter_dimension=1, tiled=True)  52.6 us
    psum x1, waiting for transfers between devices, local(): both = lax.psum(jnp.concatenate([low, grad], axis=1), 'tensor')  25.8 us
    dot_general x1, matrix products, local(): lax.dot_general(every, weight, cross, preferred_element_type=jnp.float32)  15.3 us
    dot_general x1, matrix products, local(): jnp.dot(tokens, weight, preferred_element_type=jnp.float32)  13.8 us
    dot_general x1, matrix products, local(): jnp.dot(grad_rows, down_table, preferred_element_type=jnp.float32)  9.38 us
    dot_general x1, matrix products, local(): lax.dot_general(grad_rows, tokens, along_rows, preferred_element_type=jnp...  7.08 us
    dot_general x1, matrix products, local(): lax.dot_general(tokens, down_table, cross, preferred_element_type=jnp.flo...  5.84 us
  transfers between devices with their start and end apart: 3, of which 3 were waited for; matrix products, arithmetic and copies ran while one was open for 22% of the time, Pallas kernels for 0%

profile of v1, /device:TPU:0, one launch (start us, length us, event | category | flops | bytes accessed | tf_op | source)
XLA Modules:
  0.0 227.2 jit_solution(3847694014003837904)
XLA Ops:
  7.2 0.0 all-reduce.2.cloned.1.call-start
  7.2 0.9 reduce-window.8
  8.1 0.7 broadcast_add_fusion
  8.8 0.1 select_reduce_fusion
  9.0 5.8 %fusion.19 = bf16[2048,256]{0,1:T(8,128)(2,1)S(1)} fusion(bf16[2048,2048]{1,0:T(8,128)(2,1)} %param.8, bf16[256,2048]{1,0:T(8,128)(2,1)S(1)} %bitcast.17), kind=kOutput, calls=%fused_computation.49 | convolution fusion | flops 2147483648 | bytes 10485760 | tf_op jit(solution)/shard_map/dot_general | solution.py:43
  14.8 0.9 fusion.11
  15.7 0.4 fusion.10
  16.1 0.8 pad_maximum_fusion.2
  16.9 0.0 all-reduce.2.cloned.1.call-update
  17.0 0.0 all-gather.2.cloned.1.call-start
  17.0 1.2 select_convert_fusion
  18.2 0.0 all-gather.2.cloned.1.call-update
  18.3 0.2 reduce-scatter.2.cloned.1.call-start
  18.5 13.8 %convolution_convert_fusion = bf16[2048,1024]{1,0:T(8,128)(2,1)} fusion(bf16[2048,2048]{1,0:T(8,128)(2,1)} %param.8, bf16[2048,1024]{1,0:T(8,128)(2,1)} %param.9), kind=kOutput, calls=%fused_computation.1 | convolution fusion | flops 8592031744 | bytes 16777216 | tf_op jit(solution)/shard_map/dot_general | solution.py:48
  32.3 0.0 reduce-scatter.2.cloned.1.call-update
  32.3 25.8 %all-reduce.2.cloned.1.call-done = bf16[2048,128]{0,1:T(8,128)(2,1)} async-done(((bf16[2048,128]{0,1:T(8,128)(2,1)}), bf16[2048,128]{0,1:T(8,128)(2,1)}) %all-reduce.2.cloned.1.call-update) | async-done | bytes 524304 | tf_op jit(solution)/shard_map/psum | solution.py:45
  58.1 1.2 broadcast_select_fusion.9
  59.3 1.3 convolution_multiply_fusion.2
  60.6 7.1 %convolution_multiply_fusion = f32[256,2048]{1,0:T(8,128)} fusion(bf16[2048,2048]{1,0:T(8,128)(2,1)} %param.8, bf16[2048,64]{0,1:T(8,128)(2,1)S(1)} %get-tuple-element.17, bf16[2048,64]{0,1:T(8,128)(2,1)S(1)} %get-tuple-element.15, bf16[2048,64]{0,1:T(8,128)(2,1)S(1)} %get-tuple-element.13, bf16[2048,64]{0,1:T(8,128)(2,1)S(1)} %get-tuple-element.4), kind=kOutput, calls=%fused_computation.2 | convolution fusion | flops 2152202240 | bytes 11534336 | tf_op jit(solution)/shard_map/dot_general | solution.py:55
  67.7 73.1 %all-gather.2.cloned.1.call-done = bf16[2048,1024]{1,0:T(8,128)(2,1)} async-done(((bf16[2048,256]{1,0:T(8,128)(2,1)}), bf16[2048,1024]{1,0:T(8,128)(2,1)}) %all-gather.2.cloned.1.call-update) | async-done | bytes 4194320 | tf_op jit(solution)/shard_map/all_gather | solution.py:32
  140.8 15.3 %fusion.20 = f32[2048,2048]{1,0:T(8,128)} fusion(bf16[2048,1024]{1,0:T(8,128)(2,1)} %all-gather.2.cloned.1.call-done, bf16[2048,1024]{1,0:T(8,128)(2,1)} %param.9), kind=kOutput, calls=%fused_computation.50 | convolution fusion | flops 8589934592 | bytes 25165824 | tf_op jit(solution)/shard_map/dot_general | solution.py:50
  156.1 9.4 %add_convert_fusion = bf16[2048,2048]{1,0:T(8,128)(2,1)} fusion(f32[2048,2048]{1,0:T(8,128)} %fusion.20, bf16[256,2048]{1,0:T(8,128)(2,1)S(1)} %bitcast.18, bf16[2048,64]{0,1:T(8,128)(2,1)S(1)} %get-tuple-element.17, bf16[2048,64]{0,1:T(8,128)(2,1)S(1)} %get-tuple-element.15, bf16[2048,64]{0,1:T(8,128)(2,1)S(1)} %get-tuple-element.13, ...), kind=kOutput, calls=%fused_computation | convolution fusion | flops 2164260864 | bytes 27262976 | tf_op jit(solution)/shard_map/dot_general | solution.py:53
  165.5 52.6 %reduce-scatter.2.cloned.1.call-done = bf16[2048,256]{1,0:T(8,128)(2,1)} async-done(((bf16[2048,1024]{1,0:T(8,128)(2,1)}), bf16[2048,256]{1,0:T(8,128)(2,1)}) %reduce-scatter.2.cloned.1.call-update) | async-done | bytes 1048592 | tf_op jit(solution)/shard_map/reduce_scatter | solution.py:49
  218.1 2.6 %fusion.2 = bf16[2048,256]{1,0:T(8,128)(2,1)} fusion(bf16[256,256]{1,0:T(8,128)(2,1)S(1)} %bitcast.22, bf16[2048,256]{1,0:T(8,128)(2,1)} %reduce-scatter.2.cloned.1.call-done, f32[256]{0:T(256)S(1)} %copy-done.8, pred[2048]{0:T(1024)(128)(4,1)S(1)} %get-tuple-element.24, bf16[2048,64]{0,1:T(8,128)(2,1)S(1)} %copy-done.7, bf16[2048,64]{0,1:T(8,128)(2,1)S(1)} %copy-done.5, ...), kind=kOutput, calls=%fused_computation.6 | convolution fusion | flops 275775488 | bytes 3279872 | tf_op jit(solution)/shard_map/dot_general | solution.py:65
  (23 shorter events, 0.1 us)
Async XLA Ops:
  7.2 1.8 copy-start
  7.2 50.9 %all-reduce.2.cloned.1.call-start = ((), (), s32[]{:S(2)}) async-start(), calls=%async_computation.2 | async-start | bytes 1048576 | tf_op jit(solution)/shard_map/psum | solution.py:45
  8.9 5.9 %copy-start.1 = (bf16[2048,256]{1,0:T(8,128)(2,1)S(1)}, bf16[2048,256]{1,0:T(8,128)(2,1)}, u32[]{:S(2)}) copy-start(bf16[2048,256]{1,0:T(8,128)(2,1)} %param.15) | copy-start | bytes 3145732
  8.9 5.9 %copy-start.9 = (bf16[4,64,256]{2,1,0:T(8,128)(2,1)S(1)}, bf16[4,64,256]{2,1,0:T(8,128)(2,1)}, u32[]{:S(2)}) copy-start(bf16[4,64,256]{2,1,0:T(8,128)(2,1)} %param.12) | copy-start | bytes 393220
  15.7 1.3 copy-start.8
  17.0 123.8 %all-gather.2.cloned.1.call-start = ((), (), s32[]{:S(2)}) async-start(), calls=%async_computation.3 | async-start | bytes 5242880 | tf_op jit(solution)/shard_map/all_gather | solution.py:32
  18.3 199.8 %reduce-scatter.2.cloned.1.call-start = ((), (), s32[]{:S(2)}) async-start(), calls=%async_computation.1 | async-start | bytes 5242880 | tf_op jit(solution)/shard_map/reduce_scatter | solution.py:49
  59.3 1.3 copy-start.2
  59.3 1.3 copy-start.4
  59.3 1.3 copy-start.6
  156.1 62.0 %copy-start.3 = (bf16[2048,64]{0,1:T(8,128)(2,1)S(1)}, bf16[2048,64]{0,1:T(8,128)(2,1)}, u32[]{:S(2)}) copy-start(bf16[2048,64]{0,1:T(8,128)(2,1)} %copy-done.2) | copy-start | bytes 786436
  156.1 62.0 %copy-start.5 = (bf16[2048,64]{0,1:T(8,128)(2,1)S(1)}, bf16[2048,64]{0,1:T(8,128)(2,1)}, u32[]{:S(2)}) copy-start(bf16[2048,64]{0,1:T(8,128)(2,1)} %copy-done.4) | copy-start | bytes 786436
  156.1 62.0 %copy-start.7 = (bf16[2048,64]{0,1:T(8,128)(2,1)S(1)}, bf16[2048,64]{0,1:T(8,128)(2,1)}, u32[]{:S(2)}) copy-start(bf16[2048,64]{0,1:T(8,128)(2,1)} %copy-done.6) | copy-start | bytes 786436
  156.1 62.0 %copy-start.10 = (bf16[4,64,256]{2,1,0:T(8,128)(2,1)S(1)}, bf16[4,64,256]{2,1,0:T(8,128)(2,1)}, u32[]{:S(2)}) copy-start(bf16[4,64,256]{2,1,0:T(8,128)(2,1)} %param.12) | copy-start | bytes 393220
Sparse Core Ops, SparseCore 0:
  17.1 40.9 all-reduce.1
  60.2 80.5 all-gather.1
  143.1 74.9 reduce-scatter.1

commit v2 on v1

v2 whole, which is shorter than its diff:
```python
import functools

import jax
import jax.numpy as jnp
from jax import lax
from jax.experimental import pallas as pl
from jax.experimental.pallas import tpu as pltpu
from jax.sharding import PartitionSpec as P

ADAPTER_SCALE = 2.0
MACRO = 256
CHUNK = 64
LAG = 1
TILE = 512
F32 = jnp.float32
BF16 = jnp.bfloat16
CROSS = (((1,), (1,)), ((), ()))
ALONG = (((0,), (0,)), ((), ()))
MESH = pl.DeviceIdType.MESH


def own_slots(counts, job_adapter, token_rows):
    bounds = jnp.cumsum(counts)
    starts = bounds - counts
    position = lax.broadcasted_iota(jnp.int32, (token_rows, 1), 0)
    owned = (position >= starts[None, :]) & (position < bounds[None, :])
    return jnp.sum(jnp.where(owned, job_adapter[None, :] + 1, 0), axis=1, keepdims=True) - 1


def kernel(
    n,
    tokens_hbm,
    weight,
    scale,
    down,
    up,
    slot,
    cot,
    low_pick,
    grad_pick,
    lane_slot,
    mixed,
    grad_hbm,
    down_grad,
    up_grad,
    tokens,
    part,
    scaled,
    up_in,
    up_out,
    down_in,
    down_out,
    every,
    grad_buf,
    tok_sem,
    out_sem,
    up_send,
    up_recv,
    down_send,
    down_recv,
):
    me = lax.axis_index("tensor")
    rows_all, portion = tokens.shape
    width = weight.shape[1]
    own = scale.shape[1]
    macros = rows_all // MACRO
    chunks = rows_all // CHUNK
    per = MACRO // CHUNK
    last = n - 1

    def token_copy(m):
        span = pl.ds(pl.multiple_of(m * MACRO, MACRO), MACRO)
        return pltpu.make_async_copy(tokens_hbm.at[span], tokens.at[span], tok_sem.at[m])

    def out_copy(m):
        span = pl.ds(pl.multiple_of(m * MACRO, MACRO), MACRO)
        return pltpu.make_async_copy(grad_buf.at[span], grad_hbm.at[span], out_sem.at[m])

    def up_copy(c):
        span = pl.ds(pl.multiple_of(c * CHUNK, CHUNK), CHUNK)
        return pltpu.make_async_remote_copy(
            src_ref=up_out.at[span],
            dst_ref=up_in.at[span],
            send_sem=up_send.at[c],
            recv_sem=up_recv.at[c],
            device_id={"tensor": lax.rem(me + 1, n)},
            device_id_type=MESH,
        )

    def down_copy(c):
        span = pl.ds(pl.multiple_of(c * CHUNK, CHUNK), CHUNK)
        return pltpu.make_async_remote_copy(
            src_ref=down_out.at[span],
            dst_ref=down_in.at[span],
            send_sem=down_send.at[c],
            recv_sem=down_recv.at[c],
            device_id={"tensor": lax.rem(me + n - 1, n)},
            device_id_type=MESH,
        )

    for m in range(macros):
        token_copy(m).start()

    barrier = pltpu.get_barrier_semaphore()

    @pl.when(me > 0)
    def _():
        pl.semaphore_signal(
            barrier, inc=1, device_id={"tensor": lax.rem(me + n - 1, n)}, device_id_type=MESH
        )

    @pl.when(me < last)
    def _():
        pl.semaphore_signal(
            barrier, inc=1, device_id={"tensor": lax.rem(me + 1, n)}, device_id_type=MESH
        )

    inner = (me > 0) & (me < last)

    @pl.when(inner)
    def _():
        pl.semaphore_wait(barrier, 2)

    @pl.when(jnp.logical_not(inner))
    def _():
        pl.semaphore_wait(barrier, 1)

    down_grad[...] = jnp.zeros_like(down_grad)
    up_grad[...] = jnp.zeros_like(up_grad)

    def first_half(m):
        span = pl.ds(pl.multiple_of(m * MACRO, MACRO), MACRO)
        token_copy(m).wait()
        piece = tokens[span, :]
        where = slot[span, :]
        live = where >= 0
        mask = where == lane_slot[...]
        raw = jnp.where(live, cot[span, :].astype(F32), 0.0)
        scaled[span, :] = (raw * scale[...]).astype(BF16)
        low = lax.dot_general(piece, down[...], CROSS, preferred_element_type=F32)
        grad = lax.dot_general(raw.astype(BF16), up[...], CROSS, preferred_element_type=F32)
        low = jnp.where(mask, low, 0.0).astype(BF16)
        grad = jnp.where(mask, grad, 0.0).astype(BF16)
        packed = jnp.dot(low, low_pick[...], preferred_element_type=F32) + jnp.dot(
            grad, grad_pick[...], preferred_element_type=F32
        )
        part[span, width:] = packed.astype(BF16)

        @pl.loop(0, width // TILE)
        def _(j):
            cols = pl.ds(pl.multiple_of(j * TILE, TILE), TILE)
            part[span, cols] = jnp.dot(
                piece, weight[:, cols], preferred_element_type=F32
            ).astype(BF16)

    def relay(c, into, out, ahead, behind):
        span = pl.ds(pl.multiple_of(c * CHUNK, CHUNK), CHUNK)
        for j in range(n):
            cols = slice(j * own, (j + 1) * own)
            came = into[span, cols].astype(F32)
            mine = part[span, cols].astype(F32)
            value = jnp.where(
                behind(j), came, jnp.where(ahead(j), came + mine, scaled[span, :].astype(F32))
            )
            out[span, cols] = value.astype(BF16)
        out[span, width:] = (
            into[span, width:].astype(F32) + part[span, width:].astype(F32)
        ).astype(BF16)

    def second_half(m):
        span = pl.ds(pl.multiple_of(m * MACRO, MACRO), MACRO)
        where = slot[span, :]
        live = where >= 0
        mask = where == lane_slot[...]
        raw = jnp.where(live, cot[span, :], jnp.zeros((), BF16))
        packed = (
            up_in[span, width:].astype(F32)
            + down_in[span, width:].astype(F32)
            + part[span, width:].astype(F32)
        ).astype(BF16)
        low = jnp.where(
            mask, lax.dot_general(packed, low_pick[...], CROSS, preferred_element_type=F32), 0.0
        ).astype(BF16)
        grad = jnp.where(
            mask, lax.dot_general(packed, grad_pick[...], CROSS, preferred_element_type=F32), 0.0
        ).astype(BF16)
        base = jnp.zeros((MACRO, own), F32)
        for j in range(n):
            cols = slice(j * own, (j + 1) * own)
            above = down_in[span, cols].astype(F32)
            below = up_in[span, cols].astype(F32)
            mine = part[span, cols].astype(F32)
            base = jnp.where(j == me, above + below + mine, base)
            every[:, cols] = jnp.where(
                j < me, below, jnp.where(j > me, above, scaled[span, :].astype(F32))
            ).astype(BF16)
        term = jnp.dot(low, up[...], preferred_element_type=F32)
        value = (base * scale[...]).astype(BF16).astype(F32) + ADAPTER_SCALE * term
        mixed[span, :] = jnp.where(live, value, 0.0).astype(BF16)
        up_grad[...] += ADAPTER_SCALE * lax.dot_general(
            low, raw, ALONG, preferred_element_type=F32
        )

        @pl.loop(0, portion // TILE)
        def _(j):
            cols = pl.ds(pl.multiple_of(j * TILE, TILE), TILE)
            back = lax.dot_general(every[...], weight[cols, :], CROSS, preferred_element_type=F32)
            term = jnp.dot(grad, down[:, cols], preferred_element_type=F32)
            grad_buf[span, cols] = (
                back.astype(BF16).astype(F32) + ADAPTER_SCALE * term
            ).astype(BF16)
            down_grad[:, cols] += ADAPTER_SCALE * lax.dot_general(
                grad, tokens[span, cols], ALONG, preferred_element_type=F32
            )

        out_copy(m).start()

    tail = 1 + LAG * last

    @pl.loop(0, chunks + tail)
    def _(k):
        c_up = k - 1 - LAG * me
        c_down = k - 1 - LAG * (last - me)

        @pl.when((c_up >= 0) & (c_up < chunks))
        def _():
            @pl.when(me > 0)
            def _():
                up_copy(c_up).wait_recv()

            @pl.when(me == 0)
            def _():
                span = pl.ds(pl.multiple_of(c_up * CHUNK, CHUNK), CHUNK)
                up_in[span, :] = jnp.zeros((CHUNK, up_in.shape[1]), BF16)

            @pl.when(me < last)
            def _():
                relay(c_up, up_in, up_out, lambda j: j > me, lambda j: j < me)
                up_copy(c_up).start()

        @pl.when((c_down >= 0) & (c_down < chunks))
        def _():
            @pl.when(me < last)
            def _():
                down_copy(c_down).wait_recv()

            @pl.when(me == last)
            def _():
                span = pl.ds(pl.multiple_of(c_down * CHUNK, CHUNK), CHUNK)
                down_in[span, :] = jnp.zeros((CHUNK, down_in.shape[1]), BF16)

            @pl.when(me > 0)
            def _():
                relay(c_down, down_in, down_out, lambda j: j < me, lambda j: j > me)
                down_copy(c_down).start()

        @pl.when((lax.rem(k, per) == 0) & (k < chunks))
        def _():
            first_half(lax.div(k, per))

        done = k - tail + 1

        @pl.when((done > 0) & (lax.rem(jnp.maximum(done, 0), per) == 0))
        def _():
            second_half(lax.div(done, per) - 1)

    @pl.loop(0, chunks)
    def _(c):
        @pl.when(me < last)
        def _():
            up_copy(c).wait_send()

        @pl.when(me > 0)
        def _():
            down_copy(c).wait_send()

    @pl.loop(0, macros)
    def _(m):
        out_copy(m).wait()


def local(tokens, weight, dequant_scale, down_factor, up_factor, counts, job_adapter, cotangent):
    n = lax.axis_size("tensor")
    token_rows, portion = tokens.shape
    adapters, rank, _ = down_factor.shape
    out_part = up_factor.shape[2]
    width = weight.shape[1]
    slots = adapters * rank
    slot = own_slots(counts, job_adapter, token_rows)
    down_table = down_factor.reshape(slots, portion)
    up_table = up_factor.reshape(slots, out_part)
    line = jnp.arange(slots, dtype=jnp.int32)[:, None]
    lane = jnp.arange(2 * rank, dtype=jnp.int32)[None, :]
    low_pick = (line % rank == lane).astype(BF16)
    grad_pick = (line % rank + rank == lane).astype(BF16)
    lane_slot = (jnp.arange(slots, dtype=jnp.int32) // rank)[None, :]
    message = width + 2 * rank
    chunks = token_rows // CHUNK
    macros = token_rows // MACRO
    vmem = pl.BlockSpec(memory_space=pltpu.VMEM)
    hbm = pl.BlockSpec(memory_space=pl.ANY)
    mixed, token_gradient, down_gradient, up_gradient = pl.pallas_call(
        functools.partial(kernel, n),
        out_shape=(
            jax.ShapeDtypeStruct((token_rows, out_part), BF16),
            jax.ShapeDtypeStruct((token_rows, portion), BF16),
            jax.ShapeDtypeStruct((slots, portion), F32),
            jax.ShapeDtypeStruct((slots, out_part), F32),
        ),
        in_specs=[hbm] + [vmem] * 9,
        out_specs=(vmem, hbm, vmem, vmem),
        scratch_shapes=[
            pltpu.VMEM((token_rows, portion), BF16),
            pltpu.VMEM((token_rows, message), BF16),
            pltpu.VMEM((token_rows, out_part), BF16),
            pltpu.VMEM((token_rows, message), BF16),
            pltpu.VMEM((token_rows, message), BF16),
            pltpu.VMEM((token_rows, message), BF16),
            pltpu.VMEM((token_rows, message), BF16),
            pltpu.VMEM((MACRO, width), BF16),
            pltpu.VMEM((token_rows, portion), BF16),
            pltpu.SemaphoreType.DMA((macros,)),
            pltpu.SemaphoreType.DMA((macros,)),
            pltpu.SemaphoreType.DMA((chunks,)),
            pltpu.SemaphoreType.DMA((chunks,)),
            pltpu.SemaphoreType.DMA((chunks,)),
            pltpu.SemaphoreType.DMA((chunks,)),
        ],
        compiler_params=pltpu.CompilerParams(
            collective_id=0, has_side_effects=True, vmem_limit_bytes=60 * 2**20
        ),
        cost_estimate=pl.CostEstimate(
            flops=4 * token_rows * portion * (width + slots), bytes_accessed=30 * 2**20,
            transcendentals=0,
        ),
    )(
        tokens,
        weight,
        dequant_scale[None, :],
        down_table,
        up_table,
        slot,
        cotangent,
        low_pick,
        grad_pick,
        lane_slot,
    )
    return (
        mixed,
        token_gradient,
        down_gradient.reshape(adapters, rank, portion),
        up_gradient.reshape(adapters, rank, out_part),
    )


def solution(mesh):
    placed = (
        P(("groups", "job"), "tensor"),
        P("tensor", None),
        P("tensor"),
        P(("groups", "job"), None, "tensor"),
        P(("groups", "job"), None, "tensor"),
        P(("groups", "job")),
        P(("groups", "job")),
        P(("groups", "job"), "tensor"),
    )
    return jax.shard_map(
        local,
        mesh=mesh,
        in_specs=placed,
        out_specs=(
            P(("groups", "job"), "tensor"),
            P(("groups", "job"), "tensor"),
            P(("groups", "job"), None, "tensor"),
            P(("groups", "job"), None, "tensor"),
        ),
        check_vma=False,
    )
```

time: 227 us -> 189 us (0.83)
  Pallas kernels: 0 us -> 171 us
  waiting for transfers between devices: 152 us -> 0 us
  matrix products: 56.1 us -> 0 us
  local copies, waits for them, and re-layouts: 0.06 us -> 14.2 us
  between operations: 13.9 us -> 0.66 us
  other arithmetic: 5.32 us -> 2.97 us
    pallas_call x0 -> x1, Pallas kernels: none -> 171 us  [local(): pl.pallas_call(functools.partial(kernel, n), out_shape=(jax.ShapeDtypeStr...]
    all_gather x1 -> x0, waiting for transfers between devices: 73.1 us -> none  [local(): every = lax.all_gather(scaled, 'tensor', axis=1, tiled=True)]
    dot_general x8 -> x0, matrix products: 56.1 us -> none  [the longest x1 15.3 us: local(): lax.dot_general(every, weight, cross, preferred_element_type=jnp.float32)]
    reduce_scatter x1 -> x0, waiting for transfers between devices: 52.6 us -> none  [local(): base = lax.psum_scatter(part, 'tensor', scatter_dimension=1, tiled=True)]
    psum x1 -> x0, waiting for transfers between devices: 25.8 us -> none  [local(): both = lax.psum(jnp.concatenate([low, grad], axis=1), 'tensor')]
    unnamed x22 -> x8, local copies, waits for them, and re-layouts: 0.06 us -> 12.9 us
  transfers between devices with their start and end apart: 3 -> 0, of which waited for: 3 -> 0; matrix products, arithmetic and copies ran while one was open for 22% -> 0% of each run, Pallas kernels for 0% -> 0%
where the time goes in v2:
time: 189 us
  Pallas kernels  171 us (90%)
  local copies, waits for them, and re-layouts  14.2 us (8%)
  other arithmetic  2.97 us (2%)
    pallas_call x1, Pallas kernels, local(): pl.pallas_call(functools.partial(kernel, n), out_shape=(jax.ShapeDtypeStr...  171 us
    unnamed x8, local copies, waits for them, and re-layouts  12.9 us

profile of v2, /device:TPU:0, one launch (start us, length us, event | category | flops | bytes accessed | tf_op | source)
XLA Modules:
  0.0 189.0 jit_solution(598900827570153551)
XLA Ops:
  0.6 0.8 reduce-window.8
  1.5 0.6 and_select_fusion.lane_slot
  2.0 0.7 broadcast_add_fusion.2
  2.7 0.1 select_reduce_fusion
  2.8 0.8 fusion
  3.6 1.3 copy.13.slot
  5.0 171.1 %shard_map.111 = (bf16[2048,256]{1,0:T(8,128)(2,1)}, bf16[2048,2048]{1,0:T(8,128)(2,1)}, f32[256,2048]{1,0:T(8,128)}, f32[256,256]{1,0:T(8,128)}) custom-call(bf16[2048,2048]{1,0:T(8,128)(2,1)} %tokens_hbm.1, bf16[2048,1024]{1,0:T(8,128)(2,1)} %weight.1, f32[1,256]{1,0:T(1,128)} %bitcast.16, bf16[256,2048]{1,0:T(8,128)(2,1)} %bitcast.14, ...), custom_call_target="tpu_custom_call" | custom-call | flops 21474836480 | bytes 31457280 | tf_op jit(solution)/shard_map/pallas_call | solution.py:302
  176.1 2.3 %copy.18 = bf16[2048,256]{1,0:T(8,128)(2,1)} copy(bf16[2048,256]{1,0:T(8,128)(2,1)} %get-tuple-element.20) | data formatting | bytes 2097152
  178.4 0.0 copy-start
  178.4 0.0 copy-start.1
  178.4 8.6 %copy.19 = bf16[2048,2048]{1,0:T(8,128)(2,1)} copy(bf16[2048,2048]{1,0:T(8,128)(2,1)} %get-tuple-element.21) | data formatting | bytes 16777216
  187.0 0.0 copy-done
  187.0 1.3 copy.20
  188.3 0.0 copy-done.1
  188.3 0.7 copy.21
  (3 shorter events, 0.0 us)
Async XLA Ops:
  178.4 8.6 %copy-start = (f32[256,2048]{1,0:T(8,128)S(1)}, f32[256,2048]{1,0:T(8,128)}, u32[]{:S(2)}) copy-start(f32[256,2048]{1,0:T(8,128)} %get-tuple-element.10) | copy-start | bytes 6291460
  178.4 9.9 %copy-start.1 = (f32[256,256]{1,0:T(8,128)S(1)}, f32[256,256]{1,0:T(8,128)}, u32[]{:S(2)}) copy-start(f32[256,256]{1,0:T(8,128)} %get-tuple-element.11) | copy-start | bytes 786436

commit v3 on v2

--- a/solution.py
+++ b/solution.py
@@ -2,6 +2,7 @@
 
 import jax
 import jax.numpy as jnp
+import numpy as np
 from jax import lax
 from jax.experimental import pallas as pl
 from jax.experimental.pallas import tpu as pltpu
@@ -10,21 +11,13 @@
 ADAPTER_SCALE = 2.0
 MACRO = 256
 CHUNK = 64
-LAG = 1
+LAG = 2
 TILE = 512
 F32 = jnp.float32
 BF16 = jnp.bfloat16
 CROSS = (((1,), (1,)), ((), ()))
 ALONG = (((0,), (0,)), ((), ()))
 MESH = pl.DeviceIdType.MESH
-
-
-def own_slots(counts, job_adapter, token_rows):
-    bounds = jnp.cumsum(counts)
-    starts = bounds - counts
-    position = lax.broadcasted_iota(jnp.int32, (token_rows, 1), 0)
-    owned = (position >= starts[None, :]) & (position < bounds[None, :])
-    return jnp.sum(jnp.where(owned, job_adapter[None, :] + 1, 0), axis=1, keepdims=True) - 1
 
 
 def kernel(
@@ -34,7 +27,8 @@
     scale,
     down,
     up,
-    slot,
+    counts,
+    adapters,
     cot,
     low_pick,
     grad_pick,
@@ -68,6 +62,17 @@
     per = MACRO // CHUNK
     last = n - 1
 
+    def own_slot(m):
+        position = lax.broadcasted_iota(jnp.int32, (MACRO, 1), 0) + m * MACRO
+        jobs = counts.shape[0]
+        bounds = [counts[0]]
+        for a in range(1, jobs):
+            bounds.append(bounds[-1] + counts[a])
+        found = jnp.full((MACRO, 1), -1, jnp.int32)
+        for a in reversed(range(jobs)):
+            found = jnp.where(position < bounds[a], adapters[a], found)
+        return found
+
     def token_copy(m):
         span = pl.ds(pl.multiple_of(m * MACRO, MACRO), MACRO)
         return pltpu.make_async_copy(tokens_hbm.at[span], tokens.at[span], tok_sem.at[m])
@@ -132,7 +137,7 @@
         span = pl.ds(pl.multiple_of(m * MACRO, MACRO), MACRO)
         token_copy(m).wait()
         piece = tokens[span, :]
-        where = slot[span, :]
+        where = own_slot(m)
         live = where >= 0
         mask = where == lane_slot[...]
         raw = jnp.where(live, cot[span, :].astype(F32), 0.0)
@@ -169,7 +174,7 @@
 
     def second_half(m):
         span = pl.ds(pl.multiple_of(m * MACRO, MACRO), MACRO)
-        where = slot[span, :]
+        where = own_slot(m)
         live = where >= 0
         mask = where == lane_slot[...]
         raw = jnp.where(live, cot[span, :], jnp.zeros((), BF16))
@@ -286,18 +291,18 @@
     out_part = up_factor.shape[2]
     width = weight.shape[1]
     slots = adapters * rank
-    slot = own_slots(counts, job_adapter, token_rows)
     down_table = down_factor.reshape(slots, portion)
     up_table = up_factor.reshape(slots, out_part)
-    line = jnp.arange(slots, dtype=jnp.int32)[:, None]
-    lane = jnp.arange(2 * rank, dtype=jnp.int32)[None, :]
-    low_pick = (line % rank == lane).astype(BF16)
-    grad_pick = (line % rank + rank == lane).astype(BF16)
-    lane_slot = (jnp.arange(slots, dtype=jnp.int32) // rank)[None, :]
+    line = np.arange(slots, dtype=np.int32)[:, None]
+    lane = np.arange(2 * rank, dtype=np.int32)[None, :]
+    low_pick = jnp.asarray((line % rank == lane).astype(BF16))
+    grad_pick = jnp.asarray((line % rank + rank == lane).astype(BF16))
+    lane_slot = jnp.asarray(line.T // rank)
     message = width + 2 * rank
     chunks = token_rows // CHUNK
     macros = token_rows // MACRO
     vmem = pl.BlockSpec(memory_space=pltpu.VMEM)
+    smem = pl.BlockSpec(memory_space=pltpu.SMEM)
     hbm = pl.BlockSpec(memory_space=pl.ANY)
     mixed, token_gradient, down_gradient, up_gradient = pl.pallas_call(
         functools.partial(kernel, n),
@@ -307,7 +312,7 @@
             jax.ShapeDtypeStruct((slots, portion), F32),
             jax.ShapeDtypeStruct((slots, out_part), F32),
         ),
-        in_specs=[hbm] + [vmem] * 9,
+        in_specs=[hbm] + [vmem] * 4 + [smem] * 2 + [vmem] * 4,
         out_specs=(vmem, hbm, vmem, vmem),
         scratch_shapes=[
             pltpu.VMEM((token_rows, portion), BF16),
@@ -339,7 +344,8 @@
         dequant_scale[None, :],
         down_table,
         up_table,
-        slot,
+        counts,
+        job_adapter,
         cotangent,
         low_pick,
         grad_pick,

time: 189 us -> 144 us (0.76)
  Pallas kernels: 171 us -> 130 us
  other arithmetic: 2.97 us -> 0 us
    pallas_call x1, Pallas kernels: 171 us -> 130 us  [local(): pl.pallas_call(functools.partial(kernel, n), out_shape=(jax.ShapeDtypeStr...]
where the time goes in v3:
time: 144 us; the launch traced here: 143 us
  Pallas kernels  130 us (90%)
  local copies, waits for them, and re-layouts  12.9 us (9%)
    pallas_call x1, Pallas kernels, local(): pl.pallas_call(functools.partial(kernel, n), out_shape=(jax.ShapeDtypeStr...  130 us
    unnamed x8, local copies, waits for them, and re-layouts  12.9 us

profile of v3, /device:TPU:0, one launch (start us, length us, event | category | flops | bytes accessed | tf_op | source)
XLA Modules:
  0.0 143.4 jit_solution(2747326338369125298)
XLA Ops:
  0.6 129.8 %shard_map.138 = (bf16[2048,256]{1,0:T(8,128)(2,1)}, bf16[2048,2048]{1,0:T(8,128)(2,1)}, f32[256,2048]{1,0:T(8,128)}, f32[256,256]{1,0:T(8,128)}) custom-call(bf16[2048,2048]{1,0:T(8,128)(2,1)} %tokens_hbm.1, bf16[2048,1024]{1,0:T(8,128)(2,1)} %weight.1, f32[1,256]{1,0:T(1,128)} %bitcast.9, bf16[256,2048]{1,0:T(8,128)(2,1)} %bitcast.7, ...), custom_call_target="tpu_custom_call" | custom-call | flops 21474836480 | bytes 31457280 | tf_op jit(solution)/shard_map/pallas_call | solution.py:307
  130.5 2.3 %copy.19 = bf16[2048,256]{1,0:T(8,128)(2,1)} copy(bf16[2048,256]{1,0:T(8,128)(2,1)} %get-tuple-element.16) | data formatting | bytes 2097152
  132.7 0.0 copy-start
  132.7 0.0 copy-start.1
  132.7 8.6 %copy.20 = bf16[2048,2048]{1,0:T(8,128)(2,1)} copy(bf16[2048,2048]{1,0:T(8,128)(2,1)} %get-tuple-element.17) | data formatting | bytes 16777216
  141.3 0.0 copy-done
  141.3 1.3 copy.21
  142.6 0.0 copy-done.1
  142.6 0.7 copy.22
Async XLA Ops:
  132.7 8.6 %copy-start = (f32[256,2048]{1,0:T(8,128)S(1)}, f32[256,2048]{1,0:T(8,128)}, u32[]{:S(2)}) copy-start(f32[256,2048]{1,0:T(8,128)} %get-tuple-element.10) | copy-start | bytes 6291460
  132.7 9.9 %copy-start.1 = (f32[256,256]{1,0:T(8,128)S(1)}, f32[256,256]{1,0:T(8,128)}, u32[]{:S(2)}) copy-start(f32[256,256]{1,0:T(8,128)} %get-tuple-element.11) | copy-start | bytes 786436
